TPU v7x, 128 devices: a whole 4x4x4 slice. The times are simulated.
128 devices in a mesh: ctx: 32 (over y, z, core), ch: 4 (over x).
Axes of the slice: x: 4, y: 4, z: 4, core: 2. Of those that a mesh axis runs over, the one named last changes fastest.
Arguments:
- tokens: bfloat16 [32768, 4096], P('ctx', 'ch'), may hold values from -6 to 6
- w_input: bfloat16 [2, 4096, 4096], P(None, None, 'ch'), may hold values from -0.09375 to 0.09375
- w_output: bfloat16 [4096, 4096], P('ctx', 'ch'), may hold values from -0.09375 to 0.09375
- bias_update: float32 [4096], P('ch'), may hold values from -14 to 1
- bias_cand: float32 [4096], P('ch'), may hold values from -1 to 1
- recur_gain: float32 [4096], P('ch'), may hold values from -0.95 to 0.95
- start_state: float32 [4096], P('ch'), may hold values from -1 to 1
Outputs:
- mixed: bfloat16 [32768, 4096], P('ctx', 'ch')
All inputs are finite; a program needn't handle non-finite values.
Results may differ from a plain program's by a relative error of at most 0.005.
Values may be sent and summed in bfloat16 or wider, within the bound.
A program may use at most 128 MiB of HBM per device.

v0:
```python
import math

import jax
import jax.numpy as jnp
from jax import lax
from jax.sharding import PartitionSpec as P

ITERS = 2


def scan_last(slopes, offsets):
    length = slopes.shape[-1]
    stride_len = 1
    while stride_len < length:
        lead_shape = slopes.shape[:-1] + (stride_len,)
        early_slopes = jnp.concatenate(
            [jnp.ones(lead_shape, jnp.float32), slopes[..., :-stride_len]], axis=-1
        )
        early_offsets = jnp.concatenate(
            [jnp.zeros(lead_shape, jnp.float32), offsets[..., :-stride_len]], axis=-1
        )
        offsets = slopes * early_offsets + offsets
        slopes = slopes * early_slopes
        stride_len = stride_len * 2
    return (slopes, offsets)


def block_solve(slopes, offsets):
    channels = slopes.shape[0]
    length = slopes.shape[1]
    block_len = math.gcd(length, 128)
    count = length // block_len
    inner_slope, inner_shift = scan_last(
        slopes.reshape(channels, count, block_len), offsets.reshape(channels, count, block_len)
    )
    outer_slope, outer_shift = scan_last(inner_slope[:, :, -1], inner_shift[:, :, -1])
    return (inner_slope, inner_shift, outer_slope, outer_shift)


def resolve(pieces, entering):
    inner_slope, inner_shift, outer_slope, outer_shift = pieces
    exiting = outer_slope * entering[:, None] + outer_shift
    leading = jnp.concatenate([entering[:, None], exiting[:, :-1]], axis=1)
    solved = inner_slope * leading[:, :, None] + inner_shift
    return solved.reshape(inner_slope.shape[0], -1)


def linearize(update, candidate, gain_col, previous):
    squashed = jnp.tanh(candidate + gain_col * previous)
    mapped = (1.0 - update) * previous + update * squashed
    slopes = 1.0 - update + update * gain_col * (1.0 - squashed * squashed)
    return (slopes, mapped - slopes * previous)


def on_device(tokens, w_input, w_output, bias_update, bias_cand, recur_gain, start_state):
    tok_rows = tokens.shape[0]
    chan_width = w_input.shape[2]
    gate_sums = lax.dot_general(
        w_input,
        lax.all_gather(tokens, "ch", axis=1, tiled=True),
        (((1,), (1,)), ((), ())),
        preferred_element_type=jnp.float32,
    )
    biases = jnp.stack([bias_update, bias_cand], axis=0)
    gates = (gate_sums + biases[:, :, None]).astype(jnp.bfloat16)
    groups = lax.axis_size("ctx")
    per_group = chan_width // groups
    by_group = gates.reshape(2, groups, per_group, tok_rows)
    owned_gates = lax.all_to_all(by_group, "ctx", split_axis=1, concat_axis=3, tiled=True)
    owned_gates = owned_gates.reshape(2, per_group, groups * tok_rows)
    offset_at = lax.axis_index("ctx") * per_group
    gain_col = lax.dynamic_slice_in_dim(recur_gain, offset_at, per_group, 0)[:, None]
    start_vec = lax.dynamic_slice_in_dim(start_state, offset_at, per_group, 0)
    start_col = start_vec[:, None]
    update = jax.nn.sigmoid(owned_gates[0].astype(jnp.float32))
    candidate = owned_gates[1].astype(jnp.float32)
    trajectory = jnp.zeros(candidate.shape, jnp.float32)
    for iteration in range(ITERS):
        previous = jnp.concatenate([start_col, trajectory[:, :-1]], axis=1)
        slopes, offsets = linearize(update, candidate, gain_col, previous)
        trajectory = resolve(block_solve(slopes, offsets), start_vec)
    states = trajectory.astype(jnp.bfloat16).reshape(1, per_group, groups, tok_rows)
    returned = lax.all_to_all(states, "ctx", split_axis=2, concat_axis=0, tiled=True)
    states = returned.reshape(chan_width, tok_rows)
    states_full = lax.all_gather(states, "ch", axis=0, tiled=True)
    output_sum = lax.dot_general(
        states_full,
        lax.all_gather(w_output, "ctx", axis=0, tiled=True),
        (((0,), (0,)), ((), ())),
        preferred_element_type=jnp.float32,
    )
    return output_sum.astype(jnp.bfloat16)


def solution(mesh):
    return jax.shard_map(
        on_device,
        mesh=mesh,
        in_specs=(
            P("ctx", "ch"),
            P(None, None, "ch"),
            P("ctx", "ch"),
            P("ch"),
            P("ch"),
            P("ch"),
            P("ch"),
        ),
        out_specs=P("ctx", "ch"),
        check_vma=False,
    )
```

profile of v0, /device:TPU:24, one launch (start us, length us, event | category | flops | bytes accessed | tf_op | source)
XLA Modules:
  0.0 511.0 jit_solution(17509281970817571961)
XLA Ops:
  8.8 86.3 %all-gather.4.cloned.1.call-done = bf16[1024,4096]{1,0:T(8,128)(2,1)} async-done(((bf16[1024,1024]{1,0:T(8,128)(2,1)}), bf16[1024,4096]{1,0:T(8,128)(2,1)}) %all-gather.4.cloned.1.call-update) | async-done | bytes 8388624 | tf_op jit(solution)/shard_map/all_gather | solution.py:60
  95.1 22.9 %add_convert_fusion = bf16[2,1024,1024]{2,1,0:T(8,128)(2,1)S(1)} fusion(f32[2,1024]{1,0:T(2,128)S(1)} %pad_maximum_fusion.2, bf16[2,4096,1024]{2,1,0:T(8,128)(2,1)} %param.8, bf16[1024,4096]{1,0:T(8,128)(2,1)} %all-gather.4.cloned.1.call-done), kind=kOutput, calls=%fused_computation.2 | convolution fusion | flops 17184063488 | bytes 29368320 | tf_op jit(solution)/shard_map/dot_general | solution.py:58
  118.0 2.5 copy.81
  120.5 7.6 %all-to-all-start = ((bf16[2,32,32,1024]{3,2,0,1:T(8,128)(2,1)}), bf16[2,32,32,1024]{3,2,0,1:T(8,128)(2,1)}, u32[]{:S(2)}, u32[]{:S(2)}) async-start(bf16[2,32,32,1024]{3,2,0,1:T(8,128)(2,1)} %copy.81), calls=%async_computation | async-start | bytes 8388608 | tf_op jit(solution)/shard_map/all_to_all | solution.py:69
  128.8 0.8 dynamic_slice.7
  129.5 0.8 dynamic-slice_bitcast_fusion
  130.4 0.8 dynamic_slice.6
  131.1 51.2 %all-to-all-done = bf16[2,32,32,1024]{3,2,0,1:T(8,128)(2,1)} async-done(((bf16[2,32,32,1024]{3,2,0,1:T(8,128)(2,1)}), bf16[2,32,32,1024]{3,2,0,1:T(8,128)(2,1)}, u32[]{:S(2)}, u32[]{:S(2)}) %all-to-all-start) | async-done | bytes 4194336 | tf_op jit(solution)/shard_map/all_to_all | solution.py:69
  182.3 2.7 fusion.19
  185.0 2.1 fusion.18
  188.3 2.4 fusion.11
  192.2 3.2 multiply_add_fusion.15
  195.3 9.5 %multiply_add_fusion.14 = (f32[32,256,128]{2,1,0:T(8,128)}, f32[32,256,128]{2,1,0:T(8,128)}) fusion(f32[32,256,128]{2,1,0:T(8,128)} %multiply_add_fusion.15, f32[32,256,126]{2,1,0:T(8,128)} %bitcast.153, f32[32,256,127]{2,1,0:T(8,128)S(1)} %bitcast.127, f32[4,8,256,128]{3,2,1,0:T(8,128)S(1)} %copy.94), kind=kLoop, calls=%fused_computation.46 | loop fusion | flops 3145728 | bytes 25067520 | tf_op jit(solution)/shard_map/add | solution.py:22
  204.8 10.4 %multiply_add_fusion.13 = (f32[32,256,128]{2,1,0:T(8,128)S(1)}, f32[32,256,128]{2,1,0:T(8,128)}) fusion(f32[32,256,128]{2,1,0:T(8,128)} %get-tuple-element.53, f32[32,256,124]{2,1,0:T(8,128)} %bitcast.132, f32[32,256,128]{2,1,0:T(8,128)} %get-tuple-element.54, f32[32,256,126]{2,1,0:T(8,128)} %bitcast.133), kind=kLoop, calls=%fused_computation.45 | loop fusion | flops 3145728 | bytes 24969216 | tf_op jit(solution)/shard_map/add | solution.py:22
  215.2 8.9 %multiply_add_fusion.12 = (f32[32,256,128]{2,1,0:T(8,128)}, f32[32,256,128]{2,1,0:T(8,128)}) fusion(f32[32,256,128]{2,1,0:T(8,128)S(1)} %get-tuple-element.51, f32[32,256,120]{2,1,0:T(8,128)S(1)} %bitcast.134, f32[32,256,128]{2,1,0:T(8,128)} %get-tuple-element.52, f32[32,256,124]{2,1,0:T(8,128)} %bitcast.135), kind=kLoop, calls=%fused_computation.44 | loop fusion | flops 3145728 | bytes 24772608 | tf_op jit(solution)/shard_map/add | solution.py:22
  224.2 10.5 %multiply_add_fusion.11 = (f32[32,256,128]{2,1,0:T(8,128)S(1)}, f32[32,256,128]{2,1,0:T(8,128)}) fusion(f32[32,256,128]{2,1,0:T(8,128)} %get-tuple-element.49, f32[32,256,112]{2,1,0:T(8,128)} %bitcast.136, f32[32,256,128]{2,1,0:T(8,128)} %get-tuple-element.50, f32[32,256,120]{2,1,0:T(8,128)} %bitcast.137), kind=kLoop, calls=%fused_computation.43 | loop fusion | flops 3145728 | bytes 24379392 | tf_op jit(solution)/shard_map/add | solution.py:22
  234.7 8.9 %multiply_add_fusion.10 = (f32[32,256,128]{2,1,0:T(8,128)}, f32[32,256,128]{2,1,0:T(8,128)}) fusion(f32[32,256,128]{2,1,0:T(8,128)S(1)} %get-tuple-element.47, f32[32,256,96]{2,1,0:T(8,128)S(1)} %bitcast.138, f32[32,256,128]{2,1,0:T(8,128)} %get-tuple-element.48, f32[32,256,112]{2,1,0:T(8,128)} %bitcast.139), kind=kLoop, calls=%fused_computation.42 | loop fusion | flops 3145728 | bytes 23592960 | tf_op jit(solution)/shard_map/add | solution.py:22
  243.6 10.0 %multiply_add_fusion.9 = (f32[32,256,128]{2,1,0:T(8,128)}, f32[32,256,128]{2,1,0:T(8,128)S(1)}) fusion(f32[32,256,128]{2,1,0:T(8,128)} %get-tuple-element.45, f32[32,256,64]{2,1,0:T(8,128)} %bitcast.140, f32[32,256,128]{2,1,0:T(8,128)} %get-tuple-element.46, f32[32,256,96]{2,1,0:T(8,128)} %bitcast.141), kind=kLoop, calls=%fused_computation.41 | loop fusion | flops 3145728 | bytes 22020096 | tf_op jit(solution)/shard_map/add | solution.py:22
  253.6 1.1 pad_multiply_fusion.10
  254.8 1.0 copy-done
  255.8 4.4 slice_reduce_fusion.2
  261.1 1.4 multiply_add_fusion.8
  262.5 2.4 copy.101
  265.0 1.1 maximum_bitcast_fusion
  266.1 2.7 copy.97
  268.8 2.7 add_divide_fusion
  271.5 4.5 copy.82
  275.9 4.9 reshape.85
  280.8 2.1 slice_convert_fusion
  282.9 4.5 copy.83
  287.3 4.9 reshape.86
  292.3 6.0 %fusion.10 = (f32[32,256,128]{2,1,0:T(8,128)S(1)}, f32[32,256,128]{2,1,0:T(8,128)S(1)}) fusion(f32[4,8,256,128]{3,2,1,0:T(8,128)} %copy.97, f32[32,256,128]{2,1,0:T(8,128)} %reshape.85, f32[32,256,128]{2,1,0:T(8,128)} %reshape.86, f32[32]{0:T(128)S(1)} %dynamic_slice.6), kind=kLoop, calls=%fused_computation.17 | loop fusion | flops 13631488 | bytes 20971648 | tf_op jit(solution)/shard_map/sub | solution.py:52
  298.2 3.1 multiply_add_fusion.6
  301.3 8.9 %multiply_add_fusion.5 = (f32[32,256,128]{2,1,0:T(8,128)}, f32[32,256,128]{2,1,0:T(8,128)}) fusion(f32[32,256,128]{2,1,0:T(8,128)} %multiply_add_fusion.6, f32[32,256,126]{2,1,0:T(8,128)} %bitcast.154, f32[32,256,128]{2,1,0:T(8,128)S(1)} %get-tuple-element.30, f32[32,256,127]{2,1,0:T(8,128)S(1)} %bitcast.128), kind=kLoop, calls=%fused_computation.30 | loop fusion | flops 3145728 | bytes 25067520 | tf_op jit(solution)/shard_map/add | solution.py:22
  310.2 10.1 %multiply_add_fusion.4 = (f32[32,256,128]{2,1,0:T(8,128)S(1)}, f32[32,256,128]{2,1,0:T(8,128)}) fusion(f32[32,256,128]{2,1,0:T(8,128)} %get-tuple-element.27, f32[32,256,124]{2,1,0:T(8,128)} %bitcast.143, f32[32,256,128]{2,1,0:T(8,128)} %get-tuple-element.28, f32[32,256,126]{2,1,0:T(8,128)} %bitcast.144), kind=kLoop, calls=%fused_computation.29 | loop fusion | flops 3145728 | bytes 24969216 | tf_op jit(solution)/shard_map/add | solution.py:22
  320.3 8.9 %multiply_add_fusion.3 = (f32[32,256,128]{2,1,0:T(8,128)}, f32[32,256,128]{2,1,0:T(8,128)}) fusion(f32[32,256,128]{2,1,0:T(8,128)S(1)} %get-tuple-element.25, f32[32,256,120]{2,1,0:T(8,128)S(1)} %bitcast.145, f32[32,256,128]{2,1,0:T(8,128)} %get-tuple-element.26, f32[32,256,124]{2,1,0:T(8,128)} %bitcast.146), kind=kLoop, calls=%fused_computation.28 | loop fusion | flops 3145728 | bytes 24772608 | tf_op jit(solution)/shard_map/add | solution.py:22
  329.1 10.1 %multiply_add_fusion.2 = (f32[32,256,128]{2,1,0:T(8,128)S(1)}, f32[32,256,128]{2,1,0:T(8,128)}) fusion(f32[32,256,128]{2,1,0:T(8,128)} %get-tuple-element.23, f32[32,256,112]{2,1,0:T(8,128)} %bitcast.147, f32[32,256,128]{2,1,0:T(8,128)} %get-tuple-element.24, f32[32,256,120]{2,1,0:T(8,128)} %bitcast.148), kind=kLoop, calls=%fused_computation.27 | loop fusion | flops 3145728 | bytes 24379392 | tf_op jit(solution)/shard_map/add | solution.py:22
  339.2 9.3 %multiply_add_fusion.1 = (f32[32,256,128]{2,1,0:T(8,128)}, f32[32,256,128]{2,1,0:T(8,128)}) fusion(f32[32,256,128]{2,1,0:T(8,128)S(1)} %get-tuple-element.21, f32[32,256,96]{2,1,0:T(8,128)S(1)} %bitcast.149, f32[32,256,128]{2,1,0:T(8,128)} %get-tuple-element.22, f32[32,256,112]{2,1,0:T(8,128)} %bitcast.150), kind=kLoop, calls=%fused_computation.26 | loop fusion | flops 3145728 | bytes 23592960 | tf_op jit(solution)/shard_map/add | solution.py:22
  348.5 10.1 %multiply_add_fusion = (f32[32,256,128]{2,1,0:T(8,128)}, f32[32,256,128]{2,1,0:T(8,128)S(1)}) fusion(f32[32,256,128]{2,1,0:T(8,128)} %get-tuple-element.19, f32[32,256,64]{2,1,0:T(8,128)} %bitcast.151, f32[32,256,128]{2,1,0:T(8,128)} %get-tuple-element.20, f32[32,256,96]{2,1,0:T(8,128)} %bitcast.152), kind=kLoop, calls=%fused_computation.25 | loop fusion | flops 3145728 | bytes 22020096 | tf_op jit(solution)/shard_map/add | solution.py:22
  358.5 1.1 pad_multiply_fusion.3
  359.7 2.2 slice_reduce_fusion.1
  362.0 2.2 slice_reduce_fusion
  365.1 1.4 add_convert_fusion.1
  366.5 2.3 convert_element_type.46
  368.8 2.7 copy.90
  371.5 34.9 %all_to_all.30 = bf16[1,32,32,1024]{3,1,0,2:T(8,128)(2,1)} all-to-all(bf16[1,32,32,1024]{3,1,0,2:T(8,128)(2,1)S(1)} %copy.90), channel_id=1, replica_groups=mesh['ctx'=32,'ch'=4] {'ctx'}, dimensions={2} | all-to-all | bytes 4194304 | tf_op jit(solution)/shard_map/all_to_all | solution.py:83
  406.5 82.1 %all-gather.6.cloned.1.call-done = bf16[4096,1024]{1,0:T(8,128)(2,1)} async-done(((bf16[1024,1024]{1,0:T(8,128)(2,1)}), bf16[4096,1024]{1,0:T(8,128)(2,1)}) %all-gather.6.cloned.1.call-update) | async-done | bytes 8388624 | tf_op jit(solution)/shard_map/all_gather | solution.py:85
  488.6 14.7 %convolution_convert_fusion = bf16[1024,1024]{1,0:T(8,128)(2,1)} fusion(bf16[4096,1024]{1,0:T(8,128)(2,1)} %all-gather.6.cloned.1.call-done, bf16[4096,1024]{1,0:T(8,128)(2,1)} %all-gather.8.cloned.1.call-done), kind=kOutput, calls=%fused_computation.59 | convolution fusion | flops 8590983168 | bytes 18874368 | tf_op jit(solution)/shard_map/dot_general | solution.py:86
  (40 shorter events, 6.4 us)
Async XLA Ops:
  7.4 87.7 %all-gather.4.cloned.1.call-start = ((), (), s32[]{:S(2)}) async-start(), calls=%async_computation.2 | async-start | bytes 10485760 | tf_op jit(solution)/shard_map/all_gather | solution.py:60
  120.5 61.9 %all-to-all-start = ((bf16[2,32,32,1024]{3,2,0,1:T(8,128)(2,1)}), bf16[2,32,32,1024]{3,2,0,1:T(8,128)(2,1)}, u32[]{:S(2)}, u32[]{:S(2)}) async-start(bf16[2,32,32,1024]{3,2,0,1:T(8,128)(2,1)} %copy.81), calls=%async_computation | async-start | bytes 8388608 | tf_op jit(solution)/shard_map/all_to_all | solution.py:69
  128.1 278.4 %all-gather.8.cloned.1.call-start = ((), (), s32[]{:S(2)}) async-start(), calls=%async_computation.4 | async-start | bytes 8650752 | tf_op jit(solution)/shard_map/all_gather | solution.py:88
  128.7 359.9 %all-gather.6.cloned.1.call-start = ((), (), s32[]{:S(2)}) async-start(), calls=%async_computation.3 | async-start | bytes 10485760 | tf_op jit(solution)/shard_map/all_gather | solution.py:85
  253.6 2.2 copy-start
  359.7 2.3 copy-start.1
Sparse Core Ops, SparseCore 0:
  9.9 85.1 all-gather.3
Sparse Core Ops, SparseCore 1:
  130.9 81.0 all-gather.7
  406.6 82.0 all-gather.5
where the time goes:
time: 519 us; the launch traced here: 511 us
  waiting for transfers between devices  221 us (43%)
  other arithmetic  148 us (29%)
  local copies, waits for them, and re-layouts  46.3 us (9%)
  matrix products  37.6 us (7%)
  blocking collectives  34.9 us (7%)
  between operations  15.3 us (3%)
  starting transfers between devices  7.71 us (1%)
    add x28, other arithmetic, scan_last(): offsets = slopes * early_offsets + offsets  123 us
    all_gather x1, waiting for transfers between devices, on_device(): lax.all_gather(tokens, 'ch', axis=1, tiled=True)  86.3 us
    all_gather x1, waiting for transfers between devices, on_device(): states_full = lax.all_gather(states, 'ch', axis=0, tiled=True)  82.1 us
    all_to_all x1, waiting for transfers between devices, on_device(): lax.all_to_all(by_group, 'ctx', split_axis=1, concat_axis=3, tiled=True)  51.2 us
    all_to_all x1, blocking collectives, on_device(): lax.all_to_all(states, 'ctx', split_axis=2, concat_axis=0, tiled=True)  34.9 us
    dot_general x1, matrix products, on_device(): lax.dot_general(w_input, lax.all_gather(tokens, 'ch', axis=1, tiled=True)...  22.9 us
    dot_general x1, matrix products, on_device(): lax.dot_general(states_full, lax.all_gather(w_output, 'ctx', axis=0, tile...  14.7 us
  transfers between devices with their start and end apart: 4, of which 3 were waited for; matrix products, arithmetic and copies ran while one was open for 37% of the time, Pallas kernels for 0%

commit v1 on v0

v1 whole, which is shorter than its diff:
```python
import functools

import jax
import jax.numpy as jnp
from jax import lax
from jax.experimental import pallas as pl
from jax.experimental.pallas import tpu as pltpu
from jax.sharding import PartitionSpec as P

LANES = 128
SUBS = 8
CHUNKS = 4
TILE = 256
BLOCK = 16
F32 = jnp.float32
BF16 = jnp.bfloat16


def mul(index, size):
    return pl.multiple_of(index * size, size)


def kernel(
    n_ctx, n_ch, rows, width,
    tok, w_in, w_out, bias_u, bias_c, gain_ref, start_ref, out,
    x, w, wo, ubuf, cbuf, sbuf, obuf, stage, msg, inbox,
    own_send, own_recv, fwd_send, fwd_recv,
    wo_send, wo_recv, pair_send, pair_recv,
    x_sem, w_sem, wo_sem, out_sem, msg_send, msg_recv, free,
):
    me = lax.axis_index("ctx")
    col = lax.axis_index("ch")
    right = lax.rem(col + 1, n_ch)
    left = lax.rem(col + n_ch - 1, n_ch)
    far = lax.rem(col + 2, n_ch)
    sources = (col, left, right, far)
    chunk = rows // CHUNKS
    half = chunk // 2
    wo_rows = w_out.shape[0]
    pairs = n_ctx // 2
    core = lax.rem(me, 2)
    mate = me + 1 - 2 * core
    chip = lax.div(me, 2)
    tiles = width // TILE

    barrier = pltpu.get_barrier_semaphore()
    for neighbour in (left, right):
        pl.semaphore_signal(barrier, inc=1, device_id={"ch": neighbour}, device_id_type=pl.DeviceIdType.MESH)

    def greet(j, carry):
        pl.semaphore_signal(
            barrier, inc=1, device_id={"ctx": lax.rem(me + j, n_ctx)}, device_id_type=pl.DeviceIdType.MESH
        )
        return carry

    lax.fori_loop(1, n_ctx, greet, 0)
    pl.semaphore_wait(barrier, n_ctx + 1)

    def own_copy(source, way, k):
        peer = (right, left)[way]
        return pltpu.make_async_remote_copy(
            src_ref=source.at[pl.ds(mul(k, chunk), chunk), :],
            dst_ref=x.at[1 + way, pl.ds(mul(k, chunk), chunk), :],
            send_sem=own_send.at[way, k],
            recv_sem=own_recv.at[way, k],
            device_id={"ch": peer},
            device_id_type=pl.DeviceIdType.MESH,
        )

    def fwd_copy(way, k):
        peer = (right, left)[way]
        at = pl.ds(pl.multiple_of(k * chunk + way * half, half), half)
        return pltpu.make_async_remote_copy(
            src_ref=x.at[1 + way, at, :],
            dst_ref=x.at[3, at, :],
            send_sem=fwd_send.at[way, k],
            recv_sem=fwd_recv.at[way, k],
            device_id={"ch": peer},
            device_id_type=pl.DeviceIdType.MESH,
        )

    def send_own(source, k):
        own_copy(source, 0, k).start()
        own_copy(source, 1, k).start()

    def pass_on(k):
        for way in range(2):
            own_copy(x.at[0], way, k).wait_recv()
            fwd_copy(way, k).start()

    def await_far(k):
        for way in range(2):
            fwd_copy(way, k).wait_recv()

    def finish_sends(k, carry):
        for way in range(2):
            own_copy(x.at[0], way, k).wait_send()
            fwd_copy(way, k).wait_send()
        return carry

    def start_own(k, carry):
        send_own(tok, k)
        return carry

    lax.fori_loop(0, CHUNKS, start_own, 0)

    x_copy = pltpu.make_async_copy(tok, x.at[0], x_sem)
    x_copy.start()

    def w_copy(slot):
        return pltpu.make_async_copy(
            w_in.at[:, pl.ds(mul(sources[slot], width), width), :], w.at[slot], w_sem.at[slot]
        )

    for slot in range(4):
        w_copy(slot).start()

    def wo_at(owner):
        return wo.at[pl.ds(mul(owner, wo_rows), wo_rows), :]

    wo_copy = pltpu.make_async_copy(w_out, wo_at(me), wo_sem)
    wo_copy.start()

    def wo_spread(j, owner_chip):
        return pltpu.make_async_remote_copy(
            src_ref=w_out,
            dst_ref=wo_at(owner_chip * 2 + core),
            send_sem=wo_send.at[j],
            recv_sem=wo_recv.at[owner_chip],
            device_id={"ctx": j * 2 + core},
            device_id_type=pl.DeviceIdType.MESH,
        )

    def pair_copy(j, of_core):
        return pltpu.make_async_remote_copy(
            src_ref=wo_at(j * 2 + of_core),
            dst_ref=wo_at(j * 2 + of_core),
            send_sem=pair_send.at[j],
            recv_sem=pair_recv.at[j],
            device_id={"ctx": mate},
            device_id_type=pl.DeviceIdType.MESH,
        )

    def start_spread(i, carry):
        wo_spread(lax.rem(chip + i, pairs), chip).start()
        return carry

    lax.fori_loop(1, pairs, start_spread, 0)
    wo_copy.wait()
    pair_copy(chip, core).start()

    def pair_on(i, carry):
        j = lax.rem(chip + pairs - i, pairs)
        wo_spread(j, j).wait_recv()
        pair_copy(j, core).start()
        return carry

    def pair_wait(j, carry):
        pair_copy(j, 1 - core).wait_recv()
        return carry

    def pair_finish(j, carry):
        pair_copy(j, core).wait_send()
        return carry

    def spread_finish(i, carry):
        wo_spread(lax.rem(chip + i, pairs), chip).wait_send()
        return carry

    def natural(k, tile):
        return pl.ds(pl.multiple_of(k * chunk * SUBS + tile * chunk, chunk), chunk)

    def near_gates(k, carry):
        pass_on(k)
        at = pl.ds(mul(k, chunk), chunk)

        def tile_step(n, inner):
            cols = pl.ds(mul(n, TILE), TILE)
            for gate, target in ((0, sbuf), (1, obuf)):
                total = jnp.dot(x[0, at, :], w[0, gate, :, cols], preferred_element_type=F32)
                total += jnp.dot(x[1, at, :], w[1, gate, :, cols], preferred_element_type=F32)
                total += jnp.dot(x[2, at, :], w[2, gate, :, cols], preferred_element_type=F32)
                for p in range(TILE // LANES):
                    target[natural(k, n * (TILE // LANES) + p), :] = total[:, p * LANES : (p + 1) * LANES]
            return inner

        lax.fori_loop(0, tiles, tile_step, 0)
        return carry

    x_copy.wait()
    for slot in range(4):
        w_copy(slot).wait()
    lax.fori_loop(0, CHUNKS, near_gates, 0)

    gain = gain_ref[...]
    start = start_ref[...]
    first_prev = jnp.where(me == 0, start, jnp.zeros_like(start))

    def far_gates(k):
        await_far(k)
        at = pl.ds(mul(k, chunk), chunk)

        def tile_step(n, inner):
            cols = pl.ds(mul(n, TILE), TILE)
            for gate, base, bias, target in ((0, sbuf, bias_u, ubuf), (1, obuf, bias_c, cbuf)):
                total = jnp.dot(x[3, at, :], w[3, gate, :, cols], preferred_element_type=F32)
                for p in range(TILE // LANES):
                    tile = n * (TILE // LANES) + p
                    part = total[:, p * LANES : (p + 1) * LANES] + base[natural(k, tile), :]
                    part = part + bias[:, pl.ds(mul(tile, LANES), LANES)]
                    part = part.astype(BF16).astype(F32)
                    if gate == 0:
                        part = 1.0 / (1.0 + jnp.exp(-part))
                    target[pl.ds(k * chunk * SUBS + tile, chunk, stride=SUBS), :] = part
            return inner

        lax.fori_loop(0, tiles, tile_step, 0)

    def token(ref, t):
        return ref[pl.ds(mul(t, SUBS), SUBS), :]

    def put(ref, t, value):
        ref[pl.ds(mul(t, SUBS), SUBS), :] = value

    def first_block(b, carry):
        acc_s, acc_o = carry
        base = b * BLOCK
        lead = jnp.where(b == 0, first_prev, jnp.zeros_like(start))
        for i in range(BLOCK):
            update = token(ubuf, base + i)
            cand = token(cbuf, base + i)
            keep = 1.0 - update
            if i == 0:
                squashed = jnp.tanh(cand + gain * lead)
                slope = keep + update * gain * (1.0 - squashed * squashed)
                offset = keep * lead + update * squashed - slope * lead
            else:
                squashed = jnp.tanh(cand)
                slope = keep + update * gain * (1.0 - squashed * squashed)
                offset = update * squashed
            put(sbuf, base + i, slope)
            put(obuf, base + i, offset)
            acc_o = slope * acc_o + offset
            acc_s = slope * acc_s
        return acc_s, acc_o

    blocks = chunk // BLOCK

    def far_step(k, carry):
        far_gates(k)
        return lax.fori_loop(k * blocks, (k + 1) * blocks, first_block, carry)

    ident = (jnp.ones_like(start), jnp.zeros_like(start))
    carry = lax.fori_loop(0, CHUNKS - 1, far_step, ident)
    lax.fori_loop(1, pairs, pair_on, 0)
    carry = far_step(CHUNKS - 1, carry)

    def message(stage_no, source, target):
        return pltpu.make_async_remote_copy(
            src_ref=msg.at[stage_no],
            dst_ref=inbox.at[stage_no, source],
            send_sem=msg_send.at[target],
            recv_sem=msg_recv.at[stage_no, source],
            device_id={"ctx": target},
            device_id_type=pl.DeviceIdType.MESH,
        )

    def send_maps(stage_no, maps):
        msg[stage_no, pl.ds(0, SUBS), :] = maps[0]
        msg[stage_no, pl.ds(SUBS, SUBS), :] = maps[1]

        def post(d, c):
            message(stage_no, me, d).start()
            return c

        lax.fori_loop(me + 1, n_ctx, post, 0)

    def entering(stage_no):
        def take(d, h):
            message(stage_no, d, d).wait_recv()
            return inbox[stage_no, d, pl.ds(0, SUBS), :] * h + inbox[stage_no, d, pl.ds(SUBS, SUBS), :]

        return lax.fori_loop(0, me, take, start)

    def posted(stage_no):
        def done(d, c):
            message(stage_no, me, d).wait_send()
            return c

        lax.fori_loop(me + 1, n_ctx, done, 0)

    send_maps(0, carry)
    lax.fori_loop(0, CHUNKS, finish_sends, 0)
    for neighbour in (left, right):
        pl.semaphore_signal(free, inc=1, device_id={"ch": neighbour}, device_id_type=pl.DeviceIdType.MESH)
    state = entering(0)
    posted(0)

    def second_block(b, carry):
        h, acc_s, acc_o = carry
        base = b * BLOCK
        for i in range(BLOCK):
            prev = h
            h = token(sbuf, base + i) * h + token(obuf, base + i)
            update = token(ubuf, base + i)
            cand = token(cbuf, base + i)
            keep = 1.0 - update
            squashed = jnp.tanh(cand + gain * prev)
            slope = keep + update * gain * (1.0 - squashed * squashed)
            offset = keep * prev + update * squashed - slope * prev
            put(sbuf, base + i, slope)
            put(obuf, base + i, offset)
            acc_o = slope * acc_o + offset
            acc_s = slope * acc_s
        return h, acc_s, acc_o

    final = lax.fori_loop(0, CHUNKS * blocks, second_block, (state,) + ident)
    send_maps(1, final[1:])
    state = entering(1)
    posted(1)
    pl.semaphore_wait(free, 2)

    def last_block(b, h):
        base = b * BLOCK
        for i in range(BLOCK):
            h = token(sbuf, base + i) * h + token(obuf, base + i)
            put(ubuf, base + i, h)
        return h

    def last_step(k, h):
        h = lax.fori_loop(k * blocks, (k + 1) * blocks, last_block, h)
        at = pl.ds(mul(k, chunk), chunk)
        for tile in range(SUBS):
            values = ubuf[pl.ds(k * chunk * SUBS + tile, chunk, stride=SUBS), :]
            x[0, at, tile * LANES : (tile + 1) * LANES] = values.astype(BF16)
        send_own(x.at[0], k)
        return h

    lax.fori_loop(0, CHUNKS, last_step, state)
    lax.fori_loop(0, pairs, pair_wait, 0)

    def w_part(slot, cols):
        return wo[pl.ds(mul(sources[slot], width), width), cols]

    def near_out(k, carry):
        pass_on(k)
        at = pl.ds(mul(k, chunk), chunk)

        def tile_step(n, inner):
            cols = pl.ds(mul(n, TILE), TILE)
            total = jnp.dot(x[0, at, :], w_part(0, cols), preferred_element_type=F32)
            total += jnp.dot(x[1, at, :], w_part(1, cols), preferred_element_type=F32)
            total += jnp.dot(x[2, at, :], w_part(2, cols), preferred_element_type=F32)
            for p in range(TILE // LANES):
                cbuf[natural(k, n * (TILE // LANES) + p), :] = total[:, p * LANES : (p + 1) * LANES]
            return inner

        lax.fori_loop(0, tiles, tile_step, 0)
        return carry

    lax.fori_loop(0, CHUNKS, near_out, 0)

    def out_copy(k):
        at = pl.ds(mul(k, chunk), chunk)
        return pltpu.make_async_copy(stage.at[at, :], out.at[at, :], out_sem.at[k])

    def far_out(k, carry):
        await_far(k)
        at = pl.ds(mul(k, chunk), chunk)

        def tile_step(n, inner):
            cols = pl.ds(mul(n, TILE), TILE)
            total = jnp.dot(x[3, at, :], w_part(3, cols), preferred_element_type=F32)
            for p in range(TILE // LANES):
                tile = n * (TILE // LANES) + p
                part = total[:, p * LANES : (p + 1) * LANES] + cbuf[natural(k, tile), :]
                stage[at, pl.ds(mul(tile, LANES), LANES)] = part.astype(BF16)
            return inner

        lax.fori_loop(0, tiles, tile_step, 0)
        out_copy(k).start()
        return carry

    lax.fori_loop(0, CHUNKS, far_out, 0)
    lax.fori_loop(0, CHUNKS, finish_sends, 0)
    lax.fori_loop(1, pairs, spread_finish, 0)
    lax.fori_loop(0, pairs, pair_finish, 0)

    def out_wait(k, carry):
        out_copy(k).wait()
        return carry

    lax.fori_loop(0, CHUNKS, out_wait, 0)


def on_device(tokens, w_input, w_output, bias_update, bias_cand, recur_gain, start_state):
    rows, width = tokens.shape
    n_ctx = lax.axis_size("ctx")
    n_ch = lax.axis_size("ch")
    any_spec = pl.BlockSpec(memory_space=pl.ANY)
    vmem_spec = pl.BlockSpec(memory_space=pltpu.VMEM)
    dma = pltpu.SemaphoreType.DMA
    return pl.pallas_call(
        functools.partial(kernel, n_ctx, n_ch, rows, width),
        out_shape=jax.ShapeDtypeStruct((rows, width), BF16),
        in_specs=[any_spec] * 3 + [vmem_spec] * 4,
        out_specs=any_spec,
        scratch_shapes=[
            pltpu.VMEM((4, rows, width), BF16),
            pltpu.VMEM((4, 2, width, width), BF16),
            pltpu.VMEM((n_ch * width, width), BF16),
            pltpu.VMEM((rows * SUBS, LANES), F32),
            pltpu.VMEM((rows * SUBS, LANES), F32),
            pltpu.VMEM((rows * SUBS, LANES), F32),
            pltpu.VMEM((rows * SUBS, LANES), F32),
            pltpu.VMEM((rows, width), BF16),
            pltpu.VMEM((2, 2 * SUBS, LANES), F32),
            pltpu.VMEM((2, n_ctx, 2 * SUBS, LANES), F32),
            dma((2, CHUNKS)),
            dma((2, CHUNKS)),
            dma((2, CHUNKS)),
            dma((2, CHUNKS)),
            dma((n_ctx // 2,)),
            dma((n_ctx // 2,)),
            dma((n_ctx // 2,)),
            dma((n_ctx // 2,)),
            dma,
            dma((4,)),
            dma,
            dma((CHUNKS,)),
            dma((n_ctx,)),
            dma((2, n_ctx)),
            pltpu.SemaphoreType.REGULAR,
        ],
        compiler_params=pltpu.CompilerParams(
            collective_id=0, has_side_effects=True, vmem_limit_bytes=60 * 1024 * 1024
        ),
        cost_estimate=pl.CostEstimate(
            flops=6 * rows * width * width * n_ch,
            bytes_accessed=2 * (2 * rows * width + 3 * width * width * n_ch),
            transcendentals=4 * rows * width,
        ),
    )(
        tokens,
        w_input,
        w_output,
        bias_update.reshape(1, width),
        bias_cand.reshape(1, width),
        recur_gain.reshape(SUBS, LANES),
        start_state.reshape(SUBS, LANES),
    )


def solution(mesh):
    return jax.shard_map(
        on_device,
        mesh=mesh,
        in_specs=(
            P("ctx", "ch"),
            P(None, None, "ch"),
            P("ctx", "ch"),
            P("ch"),
            P("ch"),
            P("ch"),
            P("ch"),
        ),
        out_specs=P("ctx", "ch"),
        check_vma=False,
    )
```

time: 519 us -> 189 us (0.36); the launches traced: 511 us -> 189 us
  waiting for transfers between devices: 221 us -> 0 us
  Pallas kernels: 0 us -> 186 us
  other arithmetic: 148 us -> 0 us
  local copies, waits for them, and re-layouts: 46.3 us -> 3.08 us
  matrix products: 37.6 us -> 0 us
  blocking collectives: 34.9 us -> 0 us
  between operations: 15.3 us -> 0.01 us
  starting transfers between devices: 7.71 us -> 0 us
    pallas_call x0 -> x1, Pallas kernels: none -> 186 us  [on_device(): pl.pallas_call(functools.partial(kernel, n_ctx, n_ch, rows, width), out_s...]
    all_gather x3 -> x0, waiting for transfers between devices: 168 us -> none  [the longest x1 86.3 us: on_device(): lax.all_gather(tokens, 'ch', axis=1, tiled=True)]
    add x31 -> x0, other arithmetic: 125 us -> none  [the longest x28 123 us: scan_last(): offsets = slopes * early_offsets + offsets]
    all_to_all x1 -> x0, waiting for transfers between devices: 51.2 us -> none  [on_device(): lax.all_to_all(by_group, 'ctx', split_axis=1, concat_axis=3, tiled=True)]
    dot_general x2 -> x0, matrix products: 37.6 us -> none  [the longest x1 22.9 us: on_device(): lax.dot_general(w_input, lax.all_gather(tokens, 'ch', axis=1, tiled=True)...]
    all_to_all x1 -> x0, blocking collectives: 34.9 us -> none  [on_device(): lax.all_to_all(states, 'ctx', split_axis=2, concat_axis=0, tiled=True)]
    convert_element_type x4 -> x0, local copies, waits for them, and re-layouts: 14.4 us -> none  [the longest x2 9.38 us: on_device(): candidate = owned_gates[1].astype(jnp.float32)]
    div x2 -> x0, local copies, waits for them, and re-layouts: 9.34 us -> none  [on_device(): update = jax.nn.sigmoid(owned_gates[0].astype(jnp.float32))]
  transfers between devices with their start and end apart: 4 -> 0, of which waited for: 3 -> 0; matrix products, arithmetic and copies ran while one was open for 37% -> 0% of each run, Pallas kernels for 0% -> 0%
where the time goes in v1:
time: 189 us
  Pallas kernels  186 us (98%)
  local copies, waits for them, and re-layouts  3.08 us (2%)
    pallas_call x1, Pallas kernels, on_device(): pl.pallas_call(functools.partial(kernel, n_ctx, n_ch, rows, width), out_s...  186 us

profile of v1, /device:TPU:24, one launch (start us, length us, event | category | flops | bytes accessed | tf_op | source)
XLA Modules:
  0.0 188.7 jit_solution(108917615912553407)
XLA Ops:
  0.0 185.6 %shard_map.73 = bf16[1024,1024]{1,0:T(8,128)(2,1)} custom-call(bf16[1024,1024]{1,0:T(8,128)(2,1)} %tok.1, bf16[2,4096,1024]{2,1,0:T(8,128)(2,1)} %w_in.1, bf16[128,1024]{1,0:T(8,128)(2,1)} %w_out.1, f32[1,1024]{1,0:T(1,128)} %bitcast.4, f32[1,1024]{1,0:T(1,128)} %bitcast.5, f32[8,128]{1,0:T(8,128)} %bitcast.6, f32[8,128]{1,0:T(8,128)} %bitcast.7), custom_call_target="tpu_custom_call" | custom-call | flops 25769803776 | bytes 29360128 | tf_op jit(solution)/shard_map/pallas_call | solution.py:403
  185.7 3.1 %copy.9 = bf16[1024,1024]{1,0:T(8,128)(2,1)} copy(bf16[1024,1024]{1,0:T(8,128)(2,1)} %shard_map.73) | data formatting | bytes 4194304

commit v2 on v1

v2 whole, which is shorter than its diff:
```python
import functools

import jax
import jax.numpy as jnp
from jax import lax
from jax.experimental import pallas as pl
from jax.experimental.pallas import tpu as pltpu
from jax.sharding import PartitionSpec as P

LANES = 128
CHUNKS = 4
TILE = 256
BLOCK = 16
SPAN = 4
F32 = jnp.float32
BF16 = jnp.bfloat16


def mul(index, size):
    return pl.multiple_of(index * size, size)


def kernel(
    n_ctx, n_ch, rows, width,
    tok, w_in, w_out, bias_u, bias_c, gain_ref, start_ref, out,
    x, w, wo, ubuf, cbuf, sbuf, obuf, msg, inbox,
    own_send, own_recv, fwd_send, fwd_recv,
    line_send, line_recv, hop_send, hop_recv,
    row_send, row_recv, turn_send, turn_recv,
    mate_send, mate_recv, give_send, give_recv, cross_send, cross_recv,
    x_sem, w_sem, wo_sem, out_sem, msg_send, msg_recv, free,
):
    subs = width // LANES
    size = min(TILE, width)
    me = lax.axis_index("ctx")
    col = lax.axis_index("ch")
    pair = col + 1 - 2 * lax.rem(col, 2)
    across = n_ch - 1 - col
    far = lax.rem(col + 2, n_ch)
    sources = (col, pair, across, far)
    mine = lax.rem(lax.div(col + 1, 2), 2)
    chunk = rows // CHUNKS
    part_rows = chunk // 2
    pair_share = chunk * 7 // 16 // 16 * 16 or chunk // 2
    wo_rows = w_out.shape[0]
    chips = n_ctx // 2
    core = lax.rem(me, 2)
    mate = me + 1 - 2 * core
    tiles = width // size
    y_at = lax.div(me, 2 * SPAN)
    z_at = lax.rem(lax.div(me, 2), SPAN)

    def spot(f, first, second):
        first = lax.rem(first + SPAN, SPAN)
        second = lax.rem(second + SPAN, SPAN)
        y, z = (first, second) if f == 0 else (second, first)
        return (y * SPAN + z) * 2 + core

    barrier = pltpu.get_barrier_semaphore()
    for neighbour in (pair, across):
        pl.semaphore_signal(barrier, inc=1, device_id={"ch": neighbour}, device_id_type=pl.DeviceIdType.MESH)
    around = [spot(0, y_at + 1, z_at), spot(0, y_at - 1, z_at), spot(0, y_at, z_at + 1), spot(0, y_at, z_at - 1), mate]
    for neighbour in around:
        pl.semaphore_signal(barrier, inc=1, device_id={"ctx": neighbour}, device_id_type=pl.DeviceIdType.MESH)
    pl.semaphore_wait(barrier, 2 + len(around))

    def wo_piece(owner, low, count):
        return wo.at[:, pl.ds(pl.multiple_of(owner * wo_rows + low, 16), count), :]

    wo_copy = pltpu.make_async_copy(w_out, wo.at[0, pl.ds(mul(me, wo_rows), wo_rows), :], wo_sem)
    wo_copy.start()
    cross = pltpu.make_async_remote_copy(
        src_ref=w_out,
        dst_ref=wo.at[1, pl.ds(mul(me, wo_rows), wo_rows), :],
        send_sem=cross_send,
        recv_sem=cross_recv,
        device_id={"ch": pair},
        device_id_type=pl.DeviceIdType.MESH,
    )
    cross.start()

    def own_copy(source, way, k):
        peer = (pair, across)[way]
        return pltpu.make_async_remote_copy(
            src_ref=source.at[pl.ds(mul(k, chunk), chunk), :],
            dst_ref=x.at[1 + way, pl.ds(mul(k, chunk), chunk), :],
            send_sem=own_send.at[way, k],
            recv_sem=own_recv.at[way, k],
            device_id={"ch": peer},
            device_id_type=pl.DeviceIdType.MESH,
        )

    fwd_rows = (chunk - pair_share, pair_share)

    def fwd_copy(way, k):
        peer = (across, pair)[way]
        at = pl.ds(pl.multiple_of(k * chunk + way * fwd_rows[0], 16), fwd_rows[way])
        return pltpu.make_async_remote_copy(
            src_ref=x.at[1 + way, at, :],
            dst_ref=x.at[3, at, :],
            send_sem=fwd_send.at[way, k],
            recv_sem=fwd_recv.at[way, k],
            device_id={"ch": peer},
            device_id_type=pl.DeviceIdType.MESH,
        )

    def send_own(source, k):
        own_copy(source, 0, k).start()
        own_copy(source, 1, k).start()

    def pass_on(k):
        for way in range(2):
            own_copy(x.at[0], way, k).wait_recv()
            fwd_copy(way, k).start()

    def await_far(k):
        for way in range(2):
            fwd_copy(way, k).wait_recv()

    def finish_sends(k, carry):
        for way in range(2):
            own_copy(x.at[0], way, k).wait_send()
            fwd_copy(way, k).wait_send()
        return carry

    def start_own(k, carry):
        send_own(tok, k)
        return carry

    lax.fori_loop(0, CHUNKS, start_own, 0)

    x_copy = pltpu.make_async_copy(tok, x.at[0], x_sem)
    x_copy.start()

    def w_copy(slot):
        return pltpu.make_async_copy(
            w_in.at[:, pl.ds(mul(sources[slot], width), width), :], w.at[slot], w_sem.at[slot]
        )

    for slot in range(4):
        w_copy(slot).start()

    half = wo_rows // 2
    quarter = half // 2

    def line_copy(f, way):
        a, b = (y_at, z_at) if f == 0 else (z_at, y_at)
        step = 1 - 2 * way
        piece = wo_piece(me, f * half, half)
        return pltpu.make_async_remote_copy(
            src_ref=piece, dst_ref=piece,
            send_sem=line_send.at[f, way], recv_sem=line_recv.at[f, way],
            device_id={"ctx": spot(f, a + step, b)}, device_id_type=pl.DeviceIdType.MESH,
        )

    def hop_copy(f, way):
        a, b = (y_at, z_at) if f == 0 else (z_at, y_at)
        step = 1 - 2 * way
        piece = wo_piece(spot(f, a - step, b), f * half + way * quarter, quarter)
        return pltpu.make_async_remote_copy(
            src_ref=piece, dst_ref=piece,
            send_sem=hop_send.at[f, way], recv_sem=hop_recv.at[f, way],
            device_id={"ctx": spot(f, a + step, b)}, device_id_type=pl.DeviceIdType.MESH,
        )

    def row_copy(f, j, way):
        a, b = (y_at, z_at) if f == 0 else (z_at, y_at)
        step = 1 - 2 * way
        piece = wo_piece(spot(f, a + j, b), f * half, half)
        return pltpu.make_async_remote_copy(
            src_ref=piece, dst_ref=piece,
            send_sem=row_send.at[f, j, way], recv_sem=row_recv.at[f, j, way],
            device_id={"ctx": spot(f, a, b + step)}, device_id_type=pl.DeviceIdType.MESH,
        )

    def turn_copy(f, j, way):
        a, b = (y_at, z_at) if f == 0 else (z_at, y_at)
        step = 1 - 2 * way
        piece = wo_piece(spot(f, a + j, b - step), f * half + way * quarter, quarter)
        return pltpu.make_async_remote_copy(
            src_ref=piece, dst_ref=piece,
            send_sem=turn_send.at[f, j, way], recv_sem=turn_recv.at[f, j, way],
            device_id={"ctx": spot(f, a, b + step)}, device_id_type=pl.DeviceIdType.MESH,
        )

    def mate_copy(j, of_core):
        piece = wo_piece(j * 2 + of_core, 0, wo_rows)
        return pltpu.make_async_remote_copy(
            src_ref=piece, dst_ref=piece,
            send_sem=mate_send.at[j], recv_sem=mate_recv.at[j],
            device_id={"ctx": mate}, device_id_type=pl.DeviceIdType.MESH,
        )

    both = [(f, way) for f in range(2) for way in range(2)]

    def begin_lines():
        wo_copy.wait()
        cross.wait_recv()
        for f, way in both:
            line_copy(f, way).start()
        for f, way in both:
            row_copy(f, 0, way).start()

    def begin_hops():
        for f, way in both:
            line_copy(f, way).wait_recv()
            hop_copy(f, way).start()
        for j in (1, 3):
            for f, way in both:
                row_copy(f, j, way).start()

    def begin_last_row():
        for f, way in both:
            hop_copy(f, way).wait_recv()
        for f, way in both:
            row_copy(f, 2, way).start()

    def turn(j):
        for f, way in both:
            row_copy(f, j, way).wait_recv()
            turn_copy(f, j, way).start()

    def begin_mates():
        for j in range(SPAN):
            for f, way in both:
                turn_copy(f, j, way).wait_recv()

        def start_mate(j, carry):
            mate_copy(j, core).start()
            return carry

        lax.fori_loop(0, chips, start_mate, 0)

    def finish_spread():
        cross.wait_send()
        for f, way in both:
            line_copy(f, way).wait_send()
            hop_copy(f, way).wait_send()
        for j in range(SPAN):
            for f, way in both:
                row_copy(f, j, way).wait_send()
                turn_copy(f, j, way).wait_send()

        def done(j, carry):
            mate_copy(j, core).wait_send()
            return carry

        lax.fori_loop(0, chips, done, 0)

    def mate_wait(j, carry):
        mate_copy(j, 1 - core).wait_recv()
        return carry

    def natural(k, tile):
        return pl.ds(pl.multiple_of(k * chunk * subs + tile * chunk, chunk), chunk)

    def near_gates(k):
        at = pl.ds(mul(k, chunk), chunk)

        def tile_step(n, inner):
            cols = pl.ds(mul(n, size), size)
            for gate, target in ((0, sbuf), (1, obuf)):
                total = jnp.dot(x[0, at, :], w[0, gate, :, cols], preferred_element_type=F32)
                total += jnp.dot(x[1, at, :], w[1, gate, :, cols], preferred_element_type=F32)
                total += jnp.dot(x[2, at, :], w[2, gate, :, cols], preferred_element_type=F32)
                for p in range(size // LANES):
                    target[natural(k, n * (size // LANES) + p), :] = total[:, p * LANES : (p + 1) * LANES]
            return inner

        lax.fori_loop(0, tiles, tile_step, 0)

    x_copy.wait()
    for slot in range(4):
        w_copy(slot).wait()
    begin_lines()
    for k in range(CHUNKS):
        pass_on(k)
        if k == 0:
            begin_hops()
        elif k == 1:
            begin_last_row()
            turn(0)
        elif k == 2:
            turn(1)
            turn(3)
        else:
            turn(2)
        near_gates(k)

    gain = gain_ref[...]
    start = start_ref[...]
    first_prev = jnp.where(me == 0, start, jnp.zeros_like(start))

    def far_gates(k):
        await_far(k)
        at = pl.ds(mul(k, chunk), chunk)

        def tile_step(n, inner):
            cols = pl.ds(mul(n, size), size)
            for gate, base, bias, target in ((0, sbuf, bias_u, ubuf), (1, obuf, bias_c, cbuf)):
                total = jnp.dot(x[3, at, :], w[3, gate, :, cols], preferred_element_type=F32)
                for p in range(size // LANES):
                    tile = n * (size // LANES) + p
                    part = total[:, p * LANES : (p + 1) * LANES] + base[natural(k, tile), :]
                    part = part + bias[:, pl.ds(mul(tile, LANES), LANES)]
                    part = part.astype(BF16).astype(F32)
                    if gate == 0:
                        part = 1.0 / (1.0 + jnp.exp(-part))
                    target[pl.ds(k * chunk * subs + tile, chunk, stride=subs), :] = part
            return inner

        lax.fori_loop(0, tiles, tile_step, 0)

    def token(ref, t):
        return ref[pl.ds(mul(t, subs), subs), :]

    def put(ref, t, value):
        ref[pl.ds(mul(t, subs), subs), :] = value

    def first_block(b, carry):
        acc_s, acc_o = carry
        base = b * BLOCK
        lead = jnp.where(b == 0, first_prev, jnp.zeros_like(start))
        for i in range(BLOCK):
            update = token(ubuf, base + i)
            cand = token(cbuf, base + i)
            keep = 1.0 - update
            if i == 0:
                squashed = jnp.tanh(cand + gain * lead)
                slope = keep + update * gain * (1.0 - squashed * squashed)
                offset = keep * lead + update * squashed - slope * lead
            else:
                squashed = jnp.tanh(cand)
                slope = keep + update * gain * (1.0 - squashed * squashed)
                offset = update * squashed
            put(sbuf, base + i, slope)
            put(obuf, base + i, offset)
            acc_o = slope * acc_o + offset
            acc_s = slope * acc_s
        return acc_s, acc_o

    blocks = chunk // BLOCK

    def far_step(k, carry):
        far_gates(k)
        return lax.fori_loop(k * blocks, (k + 1) * blocks, first_block, carry)

    ident = (jnp.ones_like(start), jnp.zeros_like(start))
    carry = lax.fori_loop(0, CHUNKS - 1, far_step, ident)
    begin_mates()
    carry = far_step(CHUNKS - 1, carry)

    def message(stage_no, source, target):
        return pltpu.make_async_remote_copy(
            src_ref=msg.at[stage_no],
            dst_ref=inbox.at[stage_no, source],
            send_sem=msg_send.at[target],
            recv_sem=msg_recv.at[stage_no, source],
            device_id={"ctx": target},
            device_id_type=pl.DeviceIdType.MESH,
        )

    def send_maps(stage_no, maps):
        msg[stage_no, pl.ds(0, subs), :] = maps[0]
        msg[stage_no, pl.ds(subs, subs), :] = maps[1]

        def post(d, c):
            message(stage_no, me, d).start()
            return c

        lax.fori_loop(me + 1, n_ctx, post, 0)

    def entering(stage_no):
        def take(d, h):
            message(stage_no, d, d).wait_recv()
            return inbox[stage_no, d, pl.ds(0, subs), :] * h + inbox[stage_no, d, pl.ds(subs, subs), :]

        return lax.fori_loop(0, me, take, start)

    def posted(stage_no):
        def done(d, c):
            message(stage_no, me, d).wait_send()
            return c

        lax.fori_loop(me + 1, n_ctx, done, 0)

    send_maps(0, carry)
    lax.fori_loop(0, CHUNKS, finish_sends, 0)
    for neighbour in (pair, across):
        pl.semaphore_signal(free, inc=1, device_id={"ch": neighbour}, device_id_type=pl.DeviceIdType.MESH)
    state = entering(0)
    posted(0)

    def second_block(b, carry):
        h, acc_s, acc_o = carry
        base = b * BLOCK
        for i in range(BLOCK):
            prev = h
            h = token(sbuf, base + i) * h + token(obuf, base + i)
            update = token(ubuf, base + i)
            cand = token(cbuf, base + i)
            keep = 1.0 - update
            squashed = jnp.tanh(cand + gain * prev)
            slope = keep + update * gain * (1.0 - squashed * squashed)
            offset = keep * prev + update * squashed - slope * prev
            put(sbuf, base + i, slope)
            put(obuf, base + i, offset)
            acc_o = slope * acc_o + offset
            acc_s = slope * acc_s
        return h, acc_s, acc_o

    final = lax.fori_loop(0, CHUNKS * blocks, second_block, (state,) + ident)
    send_maps(1, final[1:])
    state = entering(1)
    posted(1)
    pl.semaphore_wait(free, 2)

    def last_block(b, h):
        base = b * BLOCK
        for i in range(BLOCK):
            h = token(sbuf, base + i) * h + token(obuf, base + i)
            put(ubuf, base + i, h)
        return h

    def state_copy(k, goes_across):
        at = pl.ds(mul(2 * k + jnp.where(goes_across, mine, 1 - mine), part_rows), part_rows)
        slot = jnp.where(goes_across, 1, 0)
        return pltpu.make_async_remote_copy(
            src_ref=x.at[0, at, :],
            dst_ref=x.at[1 + slot, pl.ds(mul(k, part_rows), part_rows), :],
            send_sem=own_send.at[slot, k],
            recv_sem=own_recv.at[slot, k],
            device_id={"ch": jnp.where(goes_across, across, pair)},
            device_id_type=pl.DeviceIdType.MESH,
        )

    def state_fwd(k):
        at = pl.ds(mul(k, part_rows), part_rows)
        return pltpu.make_async_remote_copy(
            src_ref=x.at[1, at, :],
            dst_ref=x.at[3, at, :],
            send_sem=fwd_send.at[0, k],
            recv_sem=fwd_recv.at[0, k],
            device_id={"ch": across},
            device_id_type=pl.DeviceIdType.MESH,
        )

    part_blocks = part_rows // BLOCK

    def last_step(c, h):
        h = lax.fori_loop(c * part_blocks, (c + 1) * part_blocks, last_block, h)
        at = pl.ds(mul(c, part_rows), part_rows)
        for tile in range(subs):
            values = ubuf[pl.ds(c * part_rows * subs + tile, part_rows, stride=subs), :]
            x[0, at, tile * LANES : (tile + 1) * LANES] = values.astype(BF16)
        state_copy(lax.div(c, 2), lax.rem(c, 2) == mine).start()
        return h

    lax.fori_loop(0, 2 * CHUNKS, last_step, state)
    lax.fori_loop(0, chips, mate_wait, 0)

    def w_part(side, slot, cols):
        return wo[side, pl.ds(mul(sources[slot], width), width), cols]

    def held(k, side, tile):
        return pl.ds(pl.multiple_of(((k * 2 + side) * subs + tile) * part_rows, part_rows), part_rows)

    def near_out(k, carry):
        state_copy(k, False).wait_recv()
        state_fwd(k).start()
        state_copy(k, True).wait_recv()
        own = pl.ds(mul(2 * k + mine, part_rows), part_rows)
        at = pl.ds(mul(k, part_rows), part_rows)

        def tile_step(n, inner):
            cols = pl.ds(mul(n, size), size)
            for side in range(2):
                total = jnp.dot(x[0, own, :], w_part(side, 0, cols), preferred_element_type=F32)
                total += jnp.dot(x[1, at, :], w_part(side, 1, cols), preferred_element_type=F32)
                total += jnp.dot(x[2, at, :], w_part(side, 2, cols), preferred_element_type=F32)
                for p in range(size // LANES):
                    cbuf[held(k, side, n * (size // LANES) + p), :] = total[:, p * LANES : (p + 1) * LANES]
            return inner

        lax.fori_loop(0, tiles, tile_step, 0)
        return carry

    lax.fori_loop(0, CHUNKS, near_out, 0)

    def out_copy(k):
        at = pl.ds(mul(k, part_rows), part_rows)
        to = pl.ds(mul(2 * k + mine, part_rows), part_rows)
        return pltpu.make_async_copy(w.at[0, 0, at, :], out.at[to, :], out_sem.at[k])

    def give_copy(k, half_at):
        at = pl.ds(mul(k, part_rows), part_rows)
        to = pl.ds(mul(2 * k + half_at, part_rows), part_rows)
        return pltpu.make_async_remote_copy(
            src_ref=w.at[0, 1, at, :],
            dst_ref=out.at[to, :],
            send_sem=give_send.at[k],
            recv_sem=give_recv.at[k],
            device_id={"ch": pair},
            device_id_type=pl.DeviceIdType.MESH,
        )

    def far_out(k, carry):
        state_fwd(k).wait_recv()
        at = pl.ds(mul(k, part_rows), part_rows)
        for side in (1, 0):

            def tile_step(n, inner):
                cols = pl.ds(mul(n, size), size)
                total = jnp.dot(x[3, at, :], w_part(side, 3, cols), preferred_element_type=F32)
                for p in range(size // LANES):
                    tile = n * (size // LANES) + p
                    part = total[:, p * LANES : (p + 1) * LANES] + cbuf[held(k, side, tile), :]
                    w[0, side, at, pl.ds(mul(tile, LANES), LANES)] = part.astype(BF16)
                return inner

            lax.fori_loop(0, tiles, tile_step, 0)
            if side == 1:
                give_copy(k, mine).start()
            else:
                out_copy(k).start()
        return carry

    lax.fori_loop(0, CHUNKS, far_out, 0)
    finish_spread()

    def last_waits(k, carry):
        state_copy(k, False).wait_send()
        state_copy(k, True).wait_send()
        state_fwd(k).wait_send()
        out_copy(k).wait()
        give_copy(k, mine).wait_send()
        give_copy(k, 1 - mine).wait_recv()
        return carry

    lax.fori_loop(0, CHUNKS, last_waits, 0)


def on_device(tokens, w_input, w_output, bias_update, bias_cand, recur_gain, start_state):
    rows, width = tokens.shape
    subs = width // LANES
    n_ctx = lax.axis_size("ctx")
    n_ch = lax.axis_size("ch")
    any_spec = pl.BlockSpec(memory_space=pl.ANY)
    vmem_spec = pl.BlockSpec(memory_space=pltpu.VMEM)
    dma = pltpu.SemaphoreType.DMA
    return pl.pallas_call(
        functools.partial(kernel, n_ctx, n_ch, rows, width),
        out_shape=jax.ShapeDtypeStruct((rows, width), BF16),
        in_specs=[any_spec] * 3 + [vmem_spec] * 4,
        out_specs=any_spec,
        scratch_shapes=[
            pltpu.VMEM((4, rows, width), BF16),
            pltpu.VMEM((4, 2, width, width), BF16),
            pltpu.VMEM((2, n_ch * width, width), BF16),
            pltpu.VMEM((rows * subs, LANES), F32),
            pltpu.VMEM((rows * subs, LANES), F32),
            pltpu.VMEM((rows * subs, LANES), F32),
            pltpu.VMEM((rows * subs, LANES), F32),
            pltpu.VMEM((2, 2 * subs, LANES), F32),
            pltpu.VMEM((2, n_ctx, 2 * subs, LANES), F32),
            dma((2, CHUNKS)),
            dma((2, CHUNKS)),
            dma((2, CHUNKS)),
            dma((2, CHUNKS)),
            dma((2, 2)),
            dma((2, 2)),
            dma((2, 2)),
            dma((2, 2)),
            dma((2, SPAN, 2)),
            dma((2, SPAN, 2)),
            dma((2, SPAN, 2)),
            dma((2, SPAN, 2)),
            dma((n_ctx // 2,)),
            dma((n_ctx // 2,)),
            dma((CHUNKS,)),
            dma((CHUNKS,)),
            dma,
            dma,
            dma,
            dma((4,)),
            dma,
            dma((CHUNKS,)),
            dma((n_ctx,)),
            dma((2, n_ctx)),
            pltpu.SemaphoreType.REGULAR,
        ],
        compiler_params=pltpu.CompilerParams(
            collective_id=0, has_side_effects=True, vmem_limit_bytes=61 * 1024 * 1024
        ),
        cost_estimate=pl.CostEstimate(
            flops=6 * rows * width * width * n_ch,
            bytes_accessed=2 * (2 * rows * width + 3 * width * width * n_ch),
            transcendentals=4 * rows * width,
        ),
    )(
        tokens,
        w_input,
        w_output,
        bias_update.reshape(1, width),
        bias_cand.reshape(1, width),
        recur_gain.reshape(subs, LANES),
        start_state.reshape(subs, LANES),
    )


def solution(mesh):
    return jax.shard_map(
        on_device,
        mesh=mesh,
        in_specs=(
            P("ctx", "ch"),
            P(None, None, "ch"),
            P("ctx", "ch"),
            P("ch"),
            P("ch"),
            P("ch"),
            P("ch"),
        ),
        out_specs=P("ctx", "ch"),
        check_vma=False,
    )
```

time: 189 us -> 161 us (0.85)
  Pallas kernels: 186 us -> 157 us
    pallas_call x1, Pallas kernels: 186 us -> 157 us  [on_device(): pl.pallas_call(functools.partial(kernel, n_ctx, n_ch, rows, width), out_s...]
where the time goes in v2:
time: 161 us; the launch traced here: 160 us
  Pallas kernels  157 us (98%)
  local copies, waits for them, and re-layouts  3.08 us (2%)
    pallas_call x1, Pallas kernels, on_device(): pl.pallas_call(functools.partial(kernel, n_ctx, n_ch, rows, width), out_s...  157 us

profile of v2, /device:TPU:24, one launch (start us, length us, event | category | flops | bytes accessed | tf_op | source)
XLA Modules:
  0.0 160.1 jit_solution(1137500106458883103)
XLA Ops:
  0.0 157.0 %shard_map.73 = bf16[1024,1024]{1,0:T(8,128)(2,1)} custom-call(bf16[1024,1024]{1,0:T(8,128)(2,1)} %tok.1, bf16[2,4096,1024]{2,1,0:T(8,128)(2,1)} %w_in.1, bf16[128,1024]{1,0:T(8,128)(2,1)} %w_out.1, f32[1,1024]{1,0:T(1,128)} %bitcast.4, f32[1,1024]{1,0:T(1,128)} %bitcast.5, f32[8,128]{1,0:T(8,128)} %bitcast.6, f32[8,128]{1,0:T(8,128)} %bitcast.7), custom_call_target="tpu_custom_call" | custom-call | flops 25769803776 | bytes 29360128 | tf_op jit(solution)/shard_map/pallas_call | solution.py:551
  157.0 3.1 %copy.9 = bf16[1024,1024]{1,0:T(8,128)(2,1)} copy(bf16[1024,1024]{1,0:T(8,128)(2,1)} %shard_map.73) | data formatting | bytes 4194304

commit v3 on v2

--- a/solution.py
+++ b/solution.py
@@ -9,6 +9,7 @@
 
 LANES = 128
 CHUNKS = 4
+FINE = 16
 TILE = 256
 BLOCK = 16
 SPAN = 4
@@ -40,8 +41,9 @@
     sources = (col, pair, across, far)
     mine = lax.rem(lax.div(col + 1, 2), 2)
     chunk = rows // CHUNKS
-    part_rows = chunk // 2
-    pair_share = chunk * 7 // 16 // 16 * 16 or chunk // 2
+    fine = rows // FINE
+    pieces = [(k * chunk, chunk, chunk * 7 // 16) for k in range(CHUNKS - 1)]
+    pieces += [(rows - chunk, chunk // 2, chunk // 4), (rows - chunk // 2, chunk // 2, chunk * 3 // 16)]
     wo_rows = w_out.shape[0]
     chips = n_ctx // 2
     core = lax.rem(me, 2)
@@ -80,21 +82,21 @@
     cross.start()
 
     def own_copy(source, way, k):
+        low, count, _ = pieces[k]
         peer = (pair, across)[way]
         return pltpu.make_async_remote_copy(
-            src_ref=source.at[pl.ds(mul(k, chunk), chunk), :],
-            dst_ref=x.at[1 + way, pl.ds(mul(k, chunk), chunk), :],
+            src_ref=source.at[pl.ds(low, count), :],
+            dst_ref=x.at[1 + way, pl.ds(low, count), :],
             send_sem=own_send.at[way, k],
             recv_sem=own_recv.at[way, k],
             device_id={"ch": peer},
             device_id_type=pl.DeviceIdType.MESH,
         )
 
-    fwd_rows = (chunk - pair_share, pair_share)
-
     def fwd_copy(way, k):
+        low, count, share = pieces[k]
         peer = (across, pair)[way]
-        at = pl.ds(pl.multiple_of(k * chunk + way * fwd_rows[0], 16), fwd_rows[way])
+        at = pl.ds(low, count - share) if way == 0 else pl.ds(low + count - share, share)
         return pltpu.make_async_remote_copy(
             src_ref=x.at[1 + way, at, :],
             dst_ref=x.at[3, at, :],
@@ -104,30 +106,18 @@
             device_id_type=pl.DeviceIdType.MESH,
         )
 
-    def send_own(source, k):
-        own_copy(source, 0, k).start()
-        own_copy(source, 1, k).start()
-
     def pass_on(k):
         for way in range(2):
-            own_copy(x.at[0], way, k).wait_recv()
+            own_copy(tok, way, k).wait_recv()
             fwd_copy(way, k).start()
 
     def await_far(k):
         for way in range(2):
             fwd_copy(way, k).wait_recv()
 
-    def finish_sends(k, carry):
+    for k in range(len(pieces)):
         for way in range(2):
-            own_copy(x.at[0], way, k).wait_send()
-            fwd_copy(way, k).wait_send()
-        return carry
-
-    def start_own(k, carry):
-        send_own(tok, k)
-        return carry
-
-    lax.fori_loop(0, CHUNKS, start_own, 0)
+            own_copy(tok, way, k).start()
 
     x_copy = pltpu.make_async_copy(tok, x.at[0], x_sem)
     x_copy.start()
@@ -183,13 +173,17 @@
             device_id={"ctx": spot(f, a, b + step)}, device_id_type=pl.DeviceIdType.MESH,
         )
 
-    def mate_copy(j, of_core):
-        piece = wo_piece(j * 2 + of_core, 0, wo_rows)
+    def mate_copy(f, owner):
+        piece = wo_piece(owner, f * half, half)
         return pltpu.make_async_remote_copy(
             src_ref=piece, dst_ref=piece,
-            send_sem=mate_send.at[j], recv_sem=mate_recv.at[j],
+            send_sem=mate_send.at[f, lax.div(owner, 2)], recv_sem=mate_recv.at[f, lax.div(owner, 2)],
             device_id={"ctx": mate}, device_id_type=pl.DeviceIdType.MESH,
         )
+
+    def share(f, first, second):
+        a, b = (y_at, z_at) if f == 0 else (z_at, y_at)
+        mate_copy(f, spot(f, a + first, b + second)).start()
 
     both = [(f, way) for f in range(2) for way in range(2)]
 
@@ -200,6 +194,8 @@
             line_copy(f, way).start()
         for f, way in both:
             row_copy(f, 0, way).start()
+        for f in range(2):
+            share(f, 0, 0)
 
     def begin_hops():
         for f, way in both:
@@ -208,28 +204,30 @@
         for j in (1, 3):
             for f, way in both:
                 row_copy(f, j, way).start()
+        for j in (1, 3):
+            for f in range(2):
+                share(f, j, 0)
 
     def begin_last_row():
         for f, way in both:
             hop_copy(f, way).wait_recv()
         for f, way in both:
             row_copy(f, 2, way).start()
+        for f in range(2):
+            share(f, 2, 0)
 
     def turn(j):
         for f, way in both:
             row_copy(f, j, way).wait_recv()
             turn_copy(f, j, way).start()
-
-    def begin_mates():
-        for j in range(SPAN):
-            for f, way in both:
-                turn_copy(f, j, way).wait_recv()
-
-        def start_mate(j, carry):
-            mate_copy(j, core).start()
-            return carry
-
-        lax.fori_loop(0, chips, start_mate, 0)
+        for f, way in both:
+            share(f, j, 2 * way - 1)
+
+    def turned(j):
+        for f, way in both:
+            turn_copy(f, j, way).wait_recv()
+        for f in range(2):
+            share(f, j, 2)
 
     def finish_spread():
         cross.wait_send()
@@ -242,20 +240,23 @@
                 turn_copy(f, j, way).wait_send()
 
         def done(j, carry):
-            mate_copy(j, core).wait_send()
+            for f in range(2):
+                mate_copy(f, 2 * j + core).wait_send()
             return carry
 
         lax.fori_loop(0, chips, done, 0)
 
     def mate_wait(j, carry):
-        mate_copy(j, 1 - core).wait_recv()
+        for f in range(2):
+            mate_copy(f, 2 * j + 1 - core).wait_recv()
         return carry
 
     def natural(k, tile):
-        return pl.ds(pl.multiple_of(k * chunk * subs + tile * chunk, chunk), chunk)
+        low, count, _ = pieces[k]
+        return pl.ds(pl.multiple_of(low * subs + tile * count, count), count)
 
     def near_gates(k):
-        at = pl.ds(mul(k, chunk), chunk)
+        at = pl.ds(pieces[k][0], pieces[k][1])
 
         def tile_step(n, inner):
             cols = pl.ds(mul(n, size), size)
@@ -273,7 +274,7 @@
     for slot in range(4):
         w_copy(slot).wait()
     begin_lines()
-    for k in range(CHUNKS):
+    for k in range(len(pieces)):
         pass_on(k)
         if k == 0:
             begin_hops()
@@ -283,7 +284,7 @@
         elif k == 2:
             turn(1)
             turn(3)
-        else:
+        elif k == 3:
             turn(2)
         near_gates(k)
 
@@ -293,7 +294,8 @@
 
     def far_gates(k):
         await_far(k)
-        at = pl.ds(mul(k, chunk), chunk)
+        low, count, _ = pieces[k]
+        at = pl.ds(low, count)
 
         def tile_step(n, inner):
             cols = pl.ds(mul(n, size), size)
@@ -306,7 +308,7 @@
                     part = part.astype(BF16).astype(F32)
                     if gate == 0:
                         part = 1.0 / (1.0 + jnp.exp(-part))
-                    target[pl.ds(k * chunk * subs + tile, chunk, stride=subs), :] = part
+                    target[pl.ds(low * subs + tile, count, stride=subs), :] = part
             return inner
 
         lax.fori_loop(0, tiles, tile_step, 0)
@@ -339,22 +341,24 @@
             acc_s = slope * acc_s
         return acc_s, acc_o
 
-    blocks = chunk // BLOCK
-
     def far_step(k, carry):
         far_gates(k)
-        return lax.fori_loop(k * blocks, (k + 1) * blocks, first_block, carry)
+        low, count, _ = pieces[k]
+        return lax.fori_loop(low // BLOCK, (low + count) // BLOCK, first_block, carry)
 
     ident = (jnp.ones_like(start), jnp.zeros_like(start))
-    carry = lax.fori_loop(0, CHUNKS - 1, far_step, ident)
-    begin_mates()
-    carry = far_step(CHUNKS - 1, carry)
+    carry = ident
+    for k in range(len(pieces)):
+        carry = far_step(k, carry)
+        if k < 2:
+            turned((0, 1)[k])
+            turned((3, 2)[k])
 
     def message(stage_no, source, target):
         return pltpu.make_async_remote_copy(
             src_ref=msg.at[stage_no],
             dst_ref=inbox.at[stage_no, source],
-            send_sem=msg_send.at[target],
+            send_sem=msg_send.at[stage_no, target],
             recv_sem=msg_recv.at[stage_no, source],
             device_id={"ctx": target},
             device_id_type=pl.DeviceIdType.MESH,
@@ -385,11 +389,13 @@
         lax.fori_loop(me + 1, n_ctx, done, 0)
 
     send_maps(0, carry)
-    lax.fori_loop(0, CHUNKS, finish_sends, 0)
+    for k in range(len(pieces)):
+        for way in range(2):
+            own_copy(tok, way, k).wait_send()
+            fwd_copy(way, k).wait_send()
     for neighbour in (pair, across):
         pl.semaphore_signal(free, inc=1, device_id={"ch": neighbour}, device_id_type=pl.DeviceIdType.MESH)
     state = entering(0)
-    posted(0)
 
     def second_block(b, carry):
         h, acc_s, acc_o = carry
@@ -409,10 +415,9 @@
             acc_s = slope * acc_s
         return h, acc_s, acc_o
 
-    final = lax.fori_loop(0, CHUNKS * blocks, second_block, (state,) + ident)
+    final = lax.fori_loop(0, rows // BLOCK, second_block, (state,) + ident)
     send_maps(1, final[1:])
     state = entering(1)
-    posted(1)
     pl.semaphore_wait(free, 2)
 
     def last_block(b, h):
@@ -422,12 +427,14 @@
             put(ubuf, base + i, h)
         return h
 
+    def sides(k, which):
+        return pl.ds(pl.multiple_of(which * (rows // 2) + k * fine, fine), fine)
+
     def state_copy(k, goes_across):
-        at = pl.ds(mul(2 * k + jnp.where(goes_across, mine, 1 - mine), part_rows), part_rows)
         slot = jnp.where(goes_across, 1, 0)
         return pltpu.make_async_remote_copy(
-            src_ref=x.at[0, at, :],
-            dst_ref=x.at[1 + slot, pl.ds(mul(k, part_rows), part_rows), :],
+            src_ref=x.at[0, sides(k, jnp.where(goes_across, mine, 1 - mine)), :],
+            dst_ref=x.at[1 + slot, pl.ds(mul(k, fine), fine), :],
             send_sem=own_send.at[slot, k],
             recv_sem=own_recv.at[slot, k],
             device_id={"ch": jnp.where(goes_across, across, pair)},
@@ -435,7 +442,7 @@
         )
 
     def state_fwd(k):
-        at = pl.ds(mul(k, part_rows), part_rows)
+        at = pl.ds(mul(k, fine), fine)
         return pltpu.make_async_remote_copy(
             src_ref=x.at[1, at, :],
             dst_ref=x.at[3, at, :],
@@ -445,32 +452,36 @@
             device_id_type=pl.DeviceIdType.MESH,
         )
 
-    part_blocks = part_rows // BLOCK
-
     def last_step(c, h):
-        h = lax.fori_loop(c * part_blocks, (c + 1) * part_blocks, last_block, h)
-        at = pl.ds(mul(c, part_rows), part_rows)
+        h = lax.fori_loop(c * (fine // BLOCK), (c + 1) * (fine // BLOCK), last_block, h)
+        at = sides(lax.div(c, 2), lax.rem(c, 2))
         for tile in range(subs):
-            values = ubuf[pl.ds(c * part_rows * subs + tile, part_rows, stride=subs), :]
+            values = ubuf[pl.ds(c * fine * subs + tile, fine, stride=subs), :]
             x[0, at, tile * LANES : (tile + 1) * LANES] = values.astype(BF16)
         state_copy(lax.div(c, 2), lax.rem(c, 2) == mine).start()
         return h
 
-    lax.fori_loop(0, 2 * CHUNKS, last_step, state)
+    lax.fori_loop(0, FINE, last_step, state)
     lax.fori_loop(0, chips, mate_wait, 0)
 
     def w_part(side, slot, cols):
         return wo[side, pl.ds(mul(sources[slot], width), width), cols]
 
     def held(k, side, tile):
-        return pl.ds(pl.multiple_of(((k * 2 + side) * subs + tile) * part_rows, part_rows), part_rows)
+        return pl.ds(pl.multiple_of(((k * 2 + side) * subs + tile) * 2 * fine, 2 * fine), 2 * fine)
+
+    def held_half(k, side, tile):
+        low = ((lax.div(k, 2) * 2 + side) * subs + tile) * 2 * fine + lax.rem(k, 2) * fine
+        return pl.ds(pl.multiple_of(low, fine), fine)
 
     def near_out(k, carry):
-        state_copy(k, False).wait_recv()
-        state_fwd(k).start()
-        state_copy(k, True).wait_recv()
-        own = pl.ds(mul(2 * k + mine, part_rows), part_rows)
-        at = pl.ds(mul(k, part_rows), part_rows)
+        for e in range(2):
+            state_copy(2 * k + e, False).wait_recv()
+            state_fwd(2 * k + e).start()
+        for e in range(2):
+            state_copy(2 * k + e, True).wait_recv()
+        own = pl.ds(pl.multiple_of(mine * (rows // 2) + k * 2 * fine, 2 * fine), 2 * fine)
+        at = pl.ds(mul(k, 2 * fine), 2 * fine)
 
         def tile_step(n, inner):
             cols = pl.ds(mul(n, size), size)
@@ -485,16 +496,16 @@
         lax.fori_loop(0, tiles, tile_step, 0)
         return carry
 
-    lax.fori_loop(0, CHUNKS, near_out, 0)
+    lax.fori_loop(0, FINE // 4, near_out, 0)
 
     def out_copy(k):
-        at = pl.ds(mul(k, part_rows), part_rows)
-        to = pl.ds(mul(2 * k + mine, part_rows), part_rows)
+        at = pl.ds(mul(k, fine), fine)
+        to = pl.ds(mul(2 * k + mine, fine), fine)
         return pltpu.make_async_copy(w.at[0, 0, at, :], out.at[to, :], out_sem.at[k])
 
     def give_copy(k, half_at):
-        at = pl.ds(mul(k, part_rows), part_rows)
-        to = pl.ds(mul(2 * k + half_at, part_rows), part_rows)
+        at = pl.ds(mul(k, fine), fine)
+        to = pl.ds(mul(2 * k + half_at, fine), fine)
         return pltpu.make_async_remote_copy(
             src_ref=w.at[0, 1, at, :],
             dst_ref=out.at[to, :],
@@ -506,7 +517,7 @@
 
     def far_out(k, carry):
         state_fwd(k).wait_recv()
-        at = pl.ds(mul(k, part_rows), part_rows)
+        at = pl.ds(mul(k, fine), fine)
         for side in (1, 0):
 
             def tile_step(n, inner):
@@ -514,7 +525,7 @@
                 total = jnp.dot(x[3, at, :], w_part(side, 3, cols), preferred_element_type=F32)
                 for p in range(size // LANES):
                     tile = n * (size // LANES) + p
-                    part = total[:, p * LANES : (p + 1) * LANES] + cbuf[held(k, side, tile), :]
+                    part = total[:, p * LANES : (p + 1) * LANES] + cbuf[held_half(k, side, tile), :]
                     w[0, side, at, pl.ds(mul(tile, LANES), LANES)] = part.astype(BF16)
                 return inner
 
@@ -525,8 +536,10 @@
                 out_copy(k).start()
         return carry
 
-    lax.fori_loop(0, CHUNKS, far_out, 0)
+    lax.fori_loop(0, FINE // 2, far_out, 0)
     finish_spread()
+    posted(0)
+    posted(1)
 
     def last_waits(k, carry):
         state_copy(k, False).wait_send()
@@ -537,7 +550,7 @@
         give_copy(k, 1 - mine).wait_recv()
         return carry
 
-    lax.fori_loop(0, CHUNKS, last_waits, 0)
+    lax.fori_loop(0, FINE // 2, last_waits, 0)
 
 
 def on_device(tokens, w_input, w_output, bias_update, bias_cand, recur_gain, start_state):
@@ -563,10 +576,10 @@
             pltpu.VMEM((rows * subs, LANES), F32),
             pltpu.VMEM((2, 2 * subs, LANES), F32),
             pltpu.VMEM((2, n_ctx, 2 * subs, LANES), F32),
-            dma((2, CHUNKS)),
-            dma((2, CHUNKS)),
-            dma((2, CHUNKS)),
-            dma((2, CHUNKS)),
+            dma((2, FINE // 2)),
+            dma((2, FINE // 2)),
+            dma((2, FINE // 2)),
+            dma((2, FINE // 2)),
             dma((2, 2)),
             dma((2, 2)),
             dma((2, 2)),
@@ -575,17 +588,17 @@
             dma((2, SPAN, 2)),
             dma((2, SPAN, 2)),
             dma((2, SPAN, 2)),
-            dma((n_ctx // 2,)),
-            dma((n_ctx // 2,)),
-            dma((CHUNKS,)),
-            dma((CHUNKS,)),
+            dma((2, n_ctx // 2)),
+            dma((2, n_ctx // 2)),
+            dma((FINE // 2,)),
+            dma((FINE // 2,)),
             dma,
             dma,
             dma,
             dma((4,)),
             dma,
-            dma((CHUNKS,)),
-            dma((n_ctx,)),
+            dma((FINE // 2,)),
+            dma((2, n_ctx)),
             dma((2, n_ctx)),
             pltpu.SemaphoreType.REGULAR,
         ],

time: 161 us -> 153 us (0.950)
  Pallas kernels: 157 us -> 149 us
    pallas_call x1, Pallas kernels: 157 us -> 149 us  [on_device(): pl.pallas_call(functools.partial(kernel, n_ctx, n_ch, rows, width), out_s...]
where the time goes in v3:
time: 153 us; the launch traced here: 152 us
  Pallas kernels  149 us (97%)
  local copies, waits for them, and re-layouts  3.08 us (2%)
    pallas_call x1, Pallas kernels, on_device(): pl.pallas_call(functools.partial(kernel, n_ctx, n_ch, rows, width), out_s...  149 us
    unnamed x1, local copies, waits for them, and re-layouts  3.08 us

profile of v3, /device:TPU:24, one launch (start us, length us, event | category | flops | bytes accessed | tf_op | source)
XLA Modules:
  0.0 152.5 jit_solution(15318414199548892501)
XLA Ops:
  0.0 149.4 %shard_map.73 = bf16[1024,1024]{1,0:T(8,128)(2,1)} custom-call(bf16[1024,1024]{1,0:T(8,128)(2,1)} %tok.1, bf16[2,4096,1024]{2,1,0:T(8,128)(2,1)} %w_in.1, bf16[128,1024]{1,0:T(8,128)(2,1)} %w_out.1, f32[1,1024]{1,0:T(1,128)} %bitcast.4, f32[1,1024]{1,0:T(1,128)} %bitcast.5, f32[8,128]{1,0:T(8,128)} %bitcast.6, f32[8,128]{1,0:T(8,128)} %bitcast.7), custom_call_target="tpu_custom_call" | custom-call | flops 25769803776 | bytes 29360128 | tf_op jit(solution)/shard_map/pallas_call | solution.py:564
  149.4 3.1 %copy.9 = bf16[1024,1024]{1,0:T(8,128)(2,1)} copy(bf16[1024,1024]{1,0:T(8,128)(2,1)} %shard_map.73) | data formatting | bytes 4194304

commit v4 on v3

--- a/solution.py
+++ b/solution.py
@@ -10,6 +10,7 @@
 LANES = 128
 CHUNKS = 4
 FINE = 16
+PIECES = 8
 TILE = 256
 BLOCK = 16
 SPAN = 4
@@ -407,8 +408,9 @@
             cand = token(cbuf, base + i)
             keep = 1.0 - update
             squashed = jnp.tanh(cand + gain * prev)
-            slope = keep + update * gain * (1.0 - squashed * squashed)
-            offset = keep * prev + update * squashed - slope * prev
+            bend = update * gain * (1.0 - squashed * squashed)
+            slope = keep + bend
+            offset = update * squashed - bend * prev
             put(sbuf, base + i, slope)
             put(obuf, base + i, offset)
             acc_o = slope * acc_o + offset
@@ -553,6 +555,23 @@
     lax.fori_loop(0, FINE // 2, last_waits, 0)
 
 
+def hand_over(source, target, held, sem):
+    rows = source.shape[0] // PIECES
+
+    def piece(k, way):
+        at = pl.ds(k * rows, rows)
+        ends = (source.at[at, :], held.at[at, :], target.at[at, :])
+        return pltpu.make_async_copy(ends[way], ends[way + 1], sem.at[way, k])
+
+    for k in range(PIECES):
+        piece(k, 0).start()
+    for k in range(PIECES):
+        piece(k, 0).wait()
+        piece(k, 1).start()
+    for k in range(PIECES):
+        piece(k, 1).wait()
+
+
 def on_device(tokens, w_input, w_output, bias_update, bias_cand, recur_gain, start_state):
     rows, width = tokens.shape
     subs = width // LANES
@@ -561,7 +580,7 @@
     any_spec = pl.BlockSpec(memory_space=pl.ANY)
     vmem_spec = pl.BlockSpec(memory_space=pltpu.VMEM)
     dma = pltpu.SemaphoreType.DMA
-    return pl.pallas_call(
+    mixed = pl.pallas_call(
         functools.partial(kernel, n_ctx, n_ch, rows, width),
         out_shape=jax.ShapeDtypeStruct((rows, width), BF16),
         in_specs=[any_spec] * 3 + [vmem_spec] * 4,
@@ -619,6 +638,13 @@
         recur_gain.reshape(subs, LANES),
         start_state.reshape(subs, LANES),
     )
+    return pl.pallas_call(
+        hand_over,
+        out_shape=jax.ShapeDtypeStruct((rows, width), BF16),
+        in_specs=[any_spec],
+        out_specs=any_spec,
+        scratch_shapes=[pltpu.VMEM((rows, width), BF16), dma((2, PIECES))],
+    )(mixed)
 
 
 def solution(mesh):

time: 153 us -> 152 us (level)
  local copies, waits for them, and re-layouts: 3.08 us -> 0 us
  Pallas kernels: 149 us -> 152 us
    unnamed x1 -> x0, local copies, waits for them, and re-layouts: 3.08 us -> none
    pallas_call x0 -> x1, Pallas kernels: none -> 2.4 us  [on_device(): pl.pallas_call(hand_over, out_shape=jax.ShapeDtypeStruct((rows, width), B...]
where the time goes in v4:
time: 152 us
  Pallas kernels  152 us (100%)
    pallas_call x1, Pallas kernels, on_device(): pl.pallas_call(functools.partial(kernel, n_ctx, n_ch, rows, width), out_s...  149 us

profile of v4, /device:TPU:24, one launch (start us, length us, event | category | flops | bytes accessed | tf_op | source)
XLA Modules:
  0.0 151.6 jit_solution(9059911674106472532)
XLA Ops:
  0.0 149.2 %shard_map.73.source = bf16[1024,1024]{1,0:T(8,128)(2,1)} custom-call(bf16[1024,1024]{1,0:T(8,128)(2,1)} %tok.1, bf16[2,4096,1024]{2,1,0:T(8,128)(2,1)} %w_in.1, bf16[128,1024]{1,0:T(8,128)(2,1)} %w_out.1, f32[1,1024]{1,0:T(1,128)} %bitcast.4, f32[1,1024]{1,0:T(1,128)} %bitcast.5, f32[8,128]{1,0:T(8,128)} %bitcast.6, f32[8,128]{1,0:T(8,128)} %bitcast.7), custom_call_target="tpu_custom_call" | custom-call | flops 25769803776 | bytes 29360128 | tf_op jit(solution)/shard_map/pallas_call | solution.py:583
  149.2 2.4 %shard_map.74 = bf16[1024,1024]{1,0:T(8,128)(2,1)} custom-call(bf16[1024,1024]{1,0:T(8,128)(2,1)} %shard_map.73.source), custom_call_target="tpu_custom_call" | custom-call | tf_op jit(solution)/shard_map/pallas_call | solution.py:641

commit v5 on v4

--- a/solution.py
+++ b/solution.py
@@ -11,8 +11,8 @@
 CHUNKS = 4
 FINE = 16
 PIECES = 8
-TILE = 256
-BLOCK = 16
+TILE = 1024
+BLOCK = 32
 SPAN = 4
 F32 = jnp.float32
 BF16 = jnp.bfloat16

time: 152 us -> 150 us (0.987)
  Pallas kernels: 152 us -> 149 us
    pallas_call x1, Pallas kernels: 149 us -> 147 us  [on_device(): pl.pallas_call(functools.partial(kernel, n_ctx, n_ch, rows, width), out_s...]
where the time goes in v5:
time: 150 us; the launch traced here: 149 us
  Pallas kernels  149 us (99%)
    pallas_call x1, Pallas kernels, on_device(): pl.pallas_call(functools.partial(kernel, n_ctx, n_ch, rows, width), out_s...  147 us

profile of v5, /device:TPU:24, one launch (start us, length us, event | category | flops | bytes accessed | tf_op | source)
XLA Modules:
  0.0 149.4 jit_solution(13630523888635770029)
XLA Ops:
  0.0 146.8 %shard_map.73.source = bf16[1024,1024]{1,0:T(8,128)(2,1)} custom-call(bf16[1024,1024]{1,0:T(8,128)(2,1)} %tok.1, bf16[2,4096,1024]{2,1,0:T(8,128)(2,1)} %w_in.1, bf16[128,1024]{1,0:T(8,128)(2,1)} %w_out.1, f32[1,1024]{1,0:T(1,128)} %bitcast.4, f32[1,1024]{1,0:T(1,128)} %bitcast.5, f32[8,128]{1,0:T(8,128)} %bitcast.6, f32[8,128]{1,0:T(8,128)} %bitcast.7), custom_call_target="tpu_custom_call" | custom-call | flops 25769803776 | bytes 29360128 | tf_op jit(solution)/shard_map/pallas_call | solution.py:583
  146.8 2.4 %shard_map.74 = bf16[1024,1024]{1,0:T(8,128)(2,1)} custom-call(bf16[1024,1024]{1,0:T(8,128)(2,1)} %shard_map.73.source), custom_call_target="tpu_custom_call" | custom-call | tf_op jit(solution)/shard_map/pallas_call | solution.py:641

commit v6 on v5

--- a/solution.py
+++ b/solution.py
@@ -390,12 +390,6 @@
         lax.fori_loop(me + 1, n_ctx, done, 0)
 
     send_maps(0, carry)
-    for k in range(len(pieces)):
-        for way in range(2):
-            own_copy(tok, way, k).wait_send()
-            fwd_copy(way, k).wait_send()
-    for neighbour in (pair, across):
-        pl.semaphore_signal(free, inc=1, device_id={"ch": neighbour}, device_id_type=pl.DeviceIdType.MESH)
     state = entering(0)
 
     def second_block(b, carry):
@@ -419,6 +413,13 @@
 
     final = lax.fori_loop(0, rows // BLOCK, second_block, (state,) + ident)
     send_maps(1, final[1:])
+    for k in range(len(pieces)):
+        for way in range(2):
+            own_copy(tok, way, k).wait_send()
+            fwd_copy(way, k).wait_send()
+    for neighbour in (pair, across):
+        pl.semaphore_signal(free, inc=1, device_id={"ch": neighbour}, device_id_type=pl.DeviceIdType.MESH)
+    lax.fori_loop(0, chips, mate_wait, 0)
     state = entering(1)
     pl.semaphore_wait(free, 2)
 
@@ -464,7 +465,6 @@
         return h
 
     lax.fori_loop(0, FINE, last_step, state)
-    lax.fori_loop(0, chips, mate_wait, 0)
 
     def w_part(side, slot, cols):
         return wo[side, pl.ds(mul(sources[slot], width), width), cols]

time: 150 us -> 150 us (level)
  no operation moved by 1% of the time
where the time goes in v6:
time: 150 us; the launch traced here: 149 us
  Pallas kernels  149 us (99%)
    pallas_call x1, Pallas kernels, on_device(): pl.pallas_call(functools.partial(kernel, n_ctx, n_ch, rows, width), out_s...  147 us

profile of v6, /device:TPU:24, one launch (start us, length us, event | category | flops | bytes accessed | tf_op | source)
XLA Modules:
  0.0 149.4 jit_solution(10432148924613260322)
XLA Ops:
  0.0 146.8 %shard_map.73.source = bf16[1024,1024]{1,0:T(8,128)(2,1)} custom-call(bf16[1024,1024]{1,0:T(8,128)(2,1)} %tok.1, bf16[2,4096,1024]{2,1,0:T(8,128)(2,1)} %w_in.1, bf16[128,1024]{1,0:T(8,128)(2,1)} %w_out.1, f32[1,1024]{1,0:T(1,128)} %bitcast.4, f32[1,1024]{1,0:T(1,128)} %bitcast.5, f32[8,128]{1,0:T(8,128)} %bitcast.6, f32[8,128]{1,0:T(8,128)} %bitcast.7), custom_call_target="tpu_custom_call" | custom-call | flops 25769803776 | bytes 29360128 | tf_op jit(solution)/shard_map/pallas_call | solution.py:583
  146.8 2.4 %shard_map.74 = bf16[1024,1024]{1,0:T(8,128)(2,1)} custom-call(bf16[1024,1024]{1,0:T(8,128)(2,1)} %shard_map.73.source), custom_call_target="tpu_custom_call" | custom-call | tf_op jit(solution)/shard_map/pallas_call | solution.py:641
